TPU v7x, 256 devices: a whole 4x4x8 slice. The times are simulated.
256 devices in a mesh: dp: 8 (over y, core), tensor: 32 (over x, z).
Axes of the slice: x: 4, y: 4, z: 8, core: 2. Of those that a mesh axis runs over, the one named last changes fastest.
Arguments:
- hidden: bfloat16 [8192, 2048], P(('dp', 'tensor')), parts along dimension 0, may hold values from -6 to 6
- norm_gain: bfloat16 [2048], replicated, may hold values from 0.099609375 to 1.8984375
- router_weight: bfloat16 [2048, 8], replicated, may hold values from -0.125 to 0.125
- kv_weight: bfloat16 [2048, 4096], P(None, 'tensor'), may hold values from -0.125 to 0.125
- query_weight: bfloat16 [2048, 16384], P(None, 'tensor'), may hold values from -0.125 to 0.125
- out_weight: bfloat16 [16384, 2048], P('tensor'), may hold values from -0.5 to 0.5
- routes: int32 [8192, 2], P('dp'), parts along dimension 0, may hold values from 0 to 7, all different within a row; in each aligned block of 1024 rows (0 to 1023, 1024 to 2047, ...) at most 384 rows name the same one
- segment_ids: int32 [8192], P('dp'), parts along dimension 0, may hold values from 0 to 3, never falling along the last dimension, each value on 1 to 512 neighbouring positions
- page_table: int32 [64], P('dp'), parts along dimension 0, may hold values from 0 to 15, as said below
- kv_cache: bfloat16 [128, 128, 4096], P('dp', None, 'tensor'), parts along dimension 0, may hold values from -6 to 6
Outputs:
- attended_out: bfloat16 [8192, 2048], P(('dp', 'tensor')), parts along dimension 0
- new_cache: bfloat16 [128, 128, 4096], P('dp', None, 'tensor'), parts along dimension 0
There are 8 independent parts, one for each index of `dp`. A program takes and returns all parts, laid end to end along the dimension named above; an argument that names none is the same for every part. Nothing has to cross between parts.
Inputs may be any that keep to these rules, and one draw needn't show every extreme that they name: `routes`: no expert is named by more than 384 tokens of a batch, and one is named by exactly 384; a token names two different experts. `segment_ids`: ids never fall along the pack; each prompt has 1 to 512 tokens and one has exactly 512. `page_table`: distinct pages.
All inputs are finite; a program needn't handle non-finite values.
Results may differ from a plain program's by a relative error of at most 0.025.
Values may be sent and summed in bfloat16 or wider, within the bound.
A program may use at most 128 MiB of HBM per device.

v0:
```python
import jax
import jax.numpy as jnp
from jax import lax
from jax.sharding import PartitionSpec as P

D = 2048
HD = 128
EA = 8
PAGE = 128


def swapped(array, axis, bit):
    return lax.ppermute(array, axis, [(i, i ^ 1 << bit) for i in range(lax.axis_size(axis))])


def normalize(hidden, norm_gain):
    values = hidden.astype(jnp.float32)
    factor = lax.rsqrt(jnp.mean(values * values, axis=-1, keepdims=True) + 1e-05)
    return (values * factor * norm_gain.astype(jnp.float32)).astype(jnp.bfloat16)


def gate_table(normed, router_weight, routes):
    logits = jnp.dot(normed, router_weight, preferred_element_type=jnp.float32)
    chosen = jnp.take_along_axis(logits, routes, axis=1)
    weights = jax.nn.softmax(chosen, axis=-1)
    expert_ids = jnp.arange(router_weight.shape[1], dtype=jnp.int32)
    onehot = (routes[:, :, None] == expert_ids[None, None, :]).astype(jnp.float32)
    return jnp.sum(weights[:, :, None] * onehot, axis=1)


def positions_of(segment_ids):
    index_row = jnp.arange(segment_ids.shape[0], dtype=jnp.int32)
    starts_here = jnp.concatenate([jnp.ones((1,), dtype=bool), segment_ids[1:] != segment_ids[:-1]])
    segment_start = lax.cummax(jnp.where(starts_here, index_row, 0), axis=0)
    return index_row - segment_start


def rotate(values, positions):
    half_width = values.shape[-1] // 2
    frequency = 10000.0 ** (-jnp.arange(half_width, dtype=jnp.float32) / half_width)
    angles = positions.astype(jnp.float32)[:, None] * frequency[None, :]
    angles = angles.reshape((values.shape[0],) + (1,) * (values.ndim - 2) + (half_width,))
    cosine = jnp.cos(angles)
    sine_part = jnp.sin(angles)
    leading = values[..., :half_width]
    trailing = values[..., half_width:]
    return jnp.concatenate(
        [leading * cosine - trailing * sine_part, trailing * cosine + leading * sine_part], axis=-1
    )


def expert_slots(routes, expert, capacity):
    is_hit = jnp.any(routes == expert, axis=1)
    running = jnp.cumsum(is_hit.astype(jnp.int32))
    placed = jnp.where(is_hit, running - 1, capacity)
    index_row = jnp.arange(routes.shape[0], dtype=jnp.int32)
    slot_tok = jnp.zeros((capacity + 1,), jnp.int32).at[placed].set(index_row)[:capacity]
    is_valid = jnp.arange(capacity, dtype=jnp.int32) < running[-1]
    return (slot_tok, is_valid)


def attend(queries, key_rows, value_rows, allowed):
    scores = jnp.dot(queries, key_rows.T, preferred_element_type=jnp.float32)
    scores = jnp.where(allowed, scores, -1e30)
    probabilities = jax.nn.softmax(scores, axis=-1).astype(jnp.bfloat16)
    return jnp.dot(probabilities, value_rows, preferred_element_type=jnp.float32)


def project_kv(normed, weight, positions, first_block):
    projected = jnp.dot(normed, weight, preferred_element_type=jnp.float32)
    block_total = weight.shape[1] // HD
    blocks = projected.reshape(normed.shape[0], block_total, HD)
    block_index = first_block + jnp.arange(block_total, dtype=jnp.int32)
    turned = rotate(blocks, positions)
    chosen = jnp.where((block_index % 2 == 0)[None, :, None], turned, blocks)
    return chosen.astype(jnp.bfloat16).reshape(normed.shape[0], weight.shape[1])


def local(
    hidden,
    norm_gain,
    router_weight,
    kv_weight,
    query_weight,
    out_weight,
    routes,
    segment_ids,
    page_table,
    kv_cache,
):
    device_index = lax.axis_index("tensor")
    token_count = routes.shape[0]
    capacity = 3 * token_count // 8
    normed = lax.all_gather(normalize(hidden, norm_gain), "tensor", axis=0, tiled=True)
    gates = gate_table(normed, router_weight, routes)
    positions = positions_of(segment_ids)
    kv_width = kv_weight.shape[1]
    block_count = kv_width // HD
    own_rows = project_kv(normed, kv_weight, positions, device_index * block_count)
    new_cache = kv_cache.at[page_table].set(own_rows.reshape(page_table.shape[0], PAGE, kv_width))
    partner_rows = swapped(own_rows, "tensor", 0)
    leading_first = device_index % 2 == 0
    head_rows = jnp.where(
        leading_first,
        jnp.concatenate([own_rows, partner_rows], axis=1),
        jnp.concatenate([partner_rows, own_rows], axis=1),
    )
    local_heads = head_rows.shape[1] // (2 * HD)
    head_rows = head_rows.reshape(token_count, local_heads, 2, HD)
    pair_count = query_weight.shape[1] // HD
    local_experts = pair_count // local_heads
    query_cols = query_weight.reshape(D, local_heads, local_experts, HD)
    index_row = jnp.arange(token_count, dtype=jnp.int32)
    scale_factor = HD ** (-0.5)
    spread = jnp.zeros((token_count, local_heads, local_experts, HD), jnp.bfloat16)
    for expert_slot in range(local_experts):
        expert = (device_index * pair_count + expert_slot) % EA
        slot_tok, is_valid = expert_slots(routes, expert, capacity)
        queries = jnp.einsum(
            "cd,dhk->chk",
            normed[slot_tok],
            query_cols[:, :, expert_slot],
            preferred_element_type=jnp.float32,
        )
        queries = (rotate(queries, positions[slot_tok]) * scale_factor).astype(jnp.bfloat16)
        allowed = (segment_ids[slot_tok][:, None] == segment_ids[None, :]) & (
            index_row[None, :] <= slot_tok[:, None]
        )
        attended = jnp.stack(
            [attend(queries[:, 0], head_rows[:, 0, 0], head_rows[:, 0, 1], allowed)], axis=1
        )
        gate_here = gates[slot_tok, expert] * is_valid.astype(jnp.float32)
        gated = (attended * gate_here[:, None, None]).astype(jnp.bfloat16)
        target = jnp.where(is_valid, slot_tok, token_count)
        spread = spread.at[target, :, expert_slot].set(gated, mode="drop")
    flat_spread = spread.reshape(token_count, pair_count * HD)
    reduced = lax.psum_scatter(
        jnp.dot(flat_spread, out_weight, preferred_element_type=jnp.float32).astype(jnp.bfloat16),
        "tensor",
        scatter_dimension=0,
        tiled=True,
    ).astype(jnp.float32)
    attended_out = (hidden.astype(jnp.float32) + reduced).astype(jnp.bfloat16)
    return (attended_out, new_cache)


def solution(mesh):
    placed = (
        P(("dp", "tensor"), None),
        P(),
        P(),
        P(None, "tensor"),
        P(None, "tensor"),
        P("tensor", None),
        P("dp", None),
        P("dp"),
        P("dp"),
        P("dp", None, "tensor"),
    )
    return jax.shard_map(
        local,
        mesh=mesh,
        in_specs=placed,
        out_specs=(P(("dp", "tensor"), None), P("dp", None, "tensor")),
        check_vma=False,
    )
```

profile of v0, /device:TPU:8, one launch (start us, length us, event | category | flops | bytes accessed | tf_op | source)
XLA Modules:
  0.0 492.1 jit_solution(13262688912807085128)
XLA Ops:
  14.0 4.3 scatter_custom_fusion.6
  19.4 3.0 gather_fusion.12
  24.5 4.3 scatter_custom_fusion.4
  32.0 3.0 gather_fusion.8
  36.9 4.3 scatter_custom_fusion.2
  42.4 1.9 gather_fusion.6
  44.3 3.0 gather_fusion.4
  48.0 4.8 scatter_custom_fusion
  55.9 3.0 gather_fusion
  58.9 3.9 copy.62
  68.1 27.8 %all-gather.2.cloned.1.call-done = bf16[1024,2048]{1,0:T(8,128)(2,1)} async-done(((bf16[32,2048]{1,0:T(8,128)(2,1)}), bf16[1024,2048]{1,0:T(8,128)(2,1)}) %all-gather.2.cloned.1.call-update) | async-done | bytes 4194320 | tf_op jit(solution)/shard_map/all_gather | solution.py:94
  95.9 7.8 %gather_fusion.13 = bf16[384,2048]{1,0:T(8,128)(2,1)} fusion(bf16[1024,2048]{1,0:T(8,128)(2,1)} %all-gather.2.cloned.1.call-done, s32[1024]{0:T(1024)S(1)} %pad_clamp_fusion), kind=kCustom, calls=%fused_computation.13 | custom fusion | bytes 3147264 | tf_op jit(solution)/shard_map/gather | solution.py:121
  103.7 2.8 convolution_bitcast_fusion
  106.5 7.8 %gather_fusion.9 = bf16[384,2048]{1,0:T(8,128)(2,1)} fusion(bf16[1024,2048]{1,0:T(8,128)(2,1)} %all-gather.2.cloned.1.call-done, s32[1024]{0:T(1024)S(1)} %pad_clamp_fusion.1), kind=kCustom, calls=%fused_computation.9 | custom fusion | bytes 3147264 | tf_op jit(solution)/shard_map/gather | solution.py:121
  114.2 2.9 convolution_bitcast_fusion.1
  117.1 3.9 fusion.110
  122.9 1.9 collective-permute-start
  126.0 12.5 %gather_fusion.16 = f32[2048]{0:T(1024)S(1)} fusion(f32[1024,8]{0,1:T(8,128)S(1)} %fusion.111, s32[2048]{0:T(1024)S(1)} %reshape.1033), kind=kCustom, calls=%fused_computation.16 | custom fusion | bytes 32768 | tf_op jit(solution)/shard_map/jit(take_along_axis)/gather | solution.py:24
  139.4 2.7 gather_fusion.15
  142.6 2.7 gather_fusion.11
  146.0 2.7 gather_fusion.7
  149.4 7.8 %gather_fusion.1 = bf16[384,2048]{1,0:T(8,128)(2,1)} fusion(bf16[1024,2048]{1,0:T(8,128)(2,1)} %all-gather.2.cloned.1.call-done, s32[1024]{0:T(1024)S(1)} %copy-done.24), kind=kCustom, calls=%fused_computation.1 | custom fusion | bytes 3147264 | tf_op jit(solution)/shard_map/gather | solution.py:121
  157.1 2.1 convolution_bitcast_fusion.3
  159.3 2.7 gather_fusion.3
  163.1 7.8 %gather_fusion.5 = bf16[384,2048]{1,0:T(8,128)(2,1)} fusion(bf16[1024,2048]{1,0:T(8,128)(2,1)} %all-gather.2.cloned.1.call-done, s32[1024]{0:T(1024)S(1)} %copy-done.22), kind=kCustom, calls=%fused_computation.5 | custom fusion | bytes 3147264 | tf_op jit(solution)/shard_map/gather | solution.py:121
  170.9 2.2 convolution_bitcast_fusion.2
  183.0 19.2 %scatter_fusion = bf16[1024,4,128]{2,1,0:T(4,128)(2,1)S(1)} fusion(bf16[1024,4,128]{2,1,0:T(4,128)(2,1)S(1)} %broadcast.766, s32[384]{0:T(512)S(1)} %copy-done.7, bf16[384,128]{1,0:T(8,128)(2,1)S(1)} %fusion.12), kind=kCustom, calls=%fused_computation.18 | custom fusion | bytes 297984 | tf_op jit(solution)/shard_map/scatter | solution.py:135
  202.2 19.7 %scatter_fusion.1 = bf16[1024,4,128]{2,1,0:T(4,128)(2,1)S(1)} fusion(bf16[1024,4,128]{2,1,0:T(4,128)(2,1)S(1)} %scatter_fusion, s32[384]{0:T(512)S(1)} %copy-done.6, bf16[384,128]{1,0:T(8,128)(2,1)S(1)} %fusion.13), kind=kCustom, calls=%fused_computation.20 | custom fusion | bytes 297984 | tf_op jit(solution)/shard_map/scatter | solution.py:135
  221.9 19.7 %scatter_fusion.2 = bf16[1024,4,128]{2,1,0:T(4,128)(2,1)S(1)} fusion(bf16[1024,4,128]{2,1,0:T(4,128)(2,1)S(1)} %scatter_fusion.1, s32[384]{0:T(512)S(1)} %copy-done.5, bf16[384,128]{1,0:T(8,128)(2,1)S(1)} %fusion.14), kind=kCustom, calls=%fused_computation.22 | custom fusion | bytes 297984 | tf_op jit(solution)/shard_map/scatter | solution.py:135
  241.6 19.6 %scatter_fusion.3 = bf16[1024,4,128]{2,1,0:T(4,128)(2,1)S(1)} fusion(bf16[1024,4,128]{2,1,0:T(4,128)(2,1)S(1)} %scatter_fusion.2, s32[384]{0:T(512)S(1)} %copy-done.4, bf16[384,128]{1,0:T(8,128)(2,1)S(1)} %fusion.15), kind=kCustom, calls=%fused_computation.24 | custom fusion | bytes 297984 | tf_op jit(solution)/shard_map/scatter | solution.py:135
  261.2 4.3 convolution_convert_fusion
  268.1 215.4 %reduce-scatter.2.cloned.1.call-done = bf16[32,2048]{1,0:T(8,128)(2,1)} async-done(((bf16[1024,2048]{1,0:T(8,128)(2,1)}), bf16[32,2048]{1,0:T(8,128)(2,1)}) %reduce-scatter.2.cloned.1.call-update) | async-done | bytes 131088 | tf_op jit(solution)/shard_map/reduce_scatter | solution.py:137
  (187 shorter events, 45.8 us)
Async XLA Ops:
  7.2 254.0 %copy-start = (bf16[512,2048]{1,0:T(8,128)(2,1)S(1)}, bf16[512,2048]{1,0:T(8,128)(2,1)}, u32[]{:S(2)}) copy-start(bf16[512,2048]{1,0:T(8,128)(2,1)} %param.15) | copy-start | bytes 6291460
  7.2 3.7 copy-start.18
  7.2 6.2 %copy-start.1 = (s32[1024]{0:T(1024)S(1)}, s32[1024]{0:T(1024)}, u32[]{:S(2)}) copy-start(s32[1024]{0:T(1024)} %param.17) | copy-start | bytes 12292
  7.2 88.7 %all-gather.2.cloned.1.call-start = ((), (), s32[]{:S(2)}) async-start(), calls=%async_computation.1 | async-start | bytes 4325376 | tf_op jit(solution)/shard_map/all_gather | solution.py:94
  10.8 472.6 %reduce-scatter.2.cloned.1.call-start = ((), (), s32[]{:S(2)}) async-start(), calls=%async_computation.2 | async-start | bytes 4325376 | tf_op jit(solution)/shard_map/reduce_scatter | solution.py:137
  42.4 4.9 %copy-start.21 = (s32[1024]{0:T(1024)}, s32[1024]{0:T(1024)S(1)}, u32[]{:S(2)}) copy-start(s32[1024]{0:T(1024)S(1)} %pad_clamp_fusion.2) | copy-start | bytes 12292
  54.0 4.9 copy-start.23
  68.1 52.9 %copy-start.29 = (f32[64]{0:T(128)}, f32[64]{0:T(128)S(1)}, u32[]{:S(2)}) copy-start(f32[64]{0:T(128)S(1)} %multiply_power_fusion) | copy-start | bytes 772
  114.2 2.9 copy-start.15
  117.1 7.7 %copy-start.3 = (bf16[1024,2048]{1,0:T(8,128)(2,1)S(1)}, bf16[1024,2048]{1,0:T(8,128)(2,1)}, u32[]{:S(2)}) copy-start(bf16[1024,2048]{1,0:T(8,128)(2,1)} %all-gather.2.cloned.1.call-done) | copy-start | bytes 12582916
  121.0 3.9 copy-start.20
  122.9 51.7 %collective-permute-start = (bf16[1024,128]{0,1:T(8,128)(2,1)}, bf16[1024,128]{0,1:T(8,128)(2,1)}, u32[]{:S(2)}, u32[]{:S(2)}) collective-permute-start(bf16[1024,128]{0,1:T(8,128)(2,1)} %fusion.18), channel_id=1, source_target_pairs={{0,1},{1,0},{2,3},{3,2},{4,5},{5,4},{6,7},{7,6},{8,9},{9,8},{10,11... | collective-permute-start | bytes 786440 | tf_op jit(solution)/shard_map/ppermute | solution.py:13
  126.0 13.2 %copy-start.19 = (s32[1024,2]{0,1:T(2,128)S(1)}, s32[1024,2]{0,1:T(2,128)}, u32[]{:S(2)}) copy-start(s32[1024,2]{0,1:T(2,128)} %param.16) | copy-start | bytes 24580
  126.0 13.3 %copy-start.8 = (s32[384]{0:T(512)S(1)}, s32[384]{0:T(512)}, u32[]{:S(2)}) copy-start(s32[384]{0:T(512)} %get-tuple-element.28) | copy-start | bytes 4612
  139.0 3.6 copy-start.9
  142.1 4.0 copy-start.10
  145.3 4.0 copy-start.24
  159.3 3.4 copy-start.28
  159.3 3.4 copy-start.30
  159.3 3.8 copy-start.22
  170.9 2.2 copy-start.17
  170.9 2.2 copy-start.25
  170.9 2.2 copy-start.26
  170.9 2.2 copy-start.27
  173.1 3.0 copy-start.2
  173.1 3.0 copy-start.31
  173.1 3.0 copy-start.35
  182.7 19.5 %copy-start.6 = (s32[384]{0:T(512)S(1)}, s32[384]{0:T(512)}, u32[]{:S(2)}) copy-start(s32[384]{0:T(512)} %fusion.83) | copy-start | bytes 4612
  183.0 38.9 %copy-start.5 = (s32[384]{0:T(512)S(1)}, s32[384]{0:T(512)}, u32[]{:S(2)}) copy-start(s32[384]{0:T(512)} %fusion.85) | copy-start | bytes 4612
  202.2 39.4 %copy-start.4 = (s32[384]{0:T(512)S(1)}, s32[384]{0:T(512)}, u32[]{:S(2)}) copy-start(s32[384]{0:T(512)} %fusion.87) | copy-start | bytes 4612
  265.5 218.0 %copy-start.12 = (bf16[32,2048]{1,0:T(8,128)(2,1)S(1)}, bf16[32,2048]{1,0:T(8,128)(2,1)}, u32[]{:S(2)}) copy-start(bf16[32,2048]{1,0:T(8,128)(2,1)} %param.10) | copy-start | bytes 393220
  268.1 217.0 %copy-start.13 = (bf16[16,128,128]{2,1,0:T(8,128)(2,1)}, bf16[16,128,128]{2,1,0:T(8,128)(2,1)S(1)}, u32[]{:S(2)}) copy-start(bf16[16,128,128]{2,1,0:T(8,128)(2,1)S(1)} %scatter_fusion.4) | copy-start | bytes 1572868
  (11 other events, 11.6 us)
Sparse Core Ops, SparseCore 0:
  11.2 84.6 all-gather.1
  265.6 217.7 reduce-scatter.1
where the time goes:
time: 498 us; the launch traced here: 492 us
  waiting for transfers between devices  243 us (49%)
  local copies, waits for them, and re-layouts  182 us (37%)
  other arithmetic  26.6 us (5%)
  matrix products  23.4 us (5%)
  between operations  15.1 us (3%)
    reduce_scatter x1, waiting for transfers between devices, local(): lax.psum_scatter(jnp.dot(flat_spread, out_weight, preferred_element_type=...  215 us
    scatter x4, local copies, waits for them, and re-layouts, local(): spread = spread.at[target, :, expert_slot].set(gated, mode='drop')  78.1 us
    gather x4, local copies, waits for them, and re-layouts, local(): normed[slot_tok]  31.1 us
    all_gather x1, waiting for transfers between devices, local(): lax.all_gather(normalize(hidden, norm_gain), 'tensor', axis=0, tiled=True)  27.8 us
    scatter x4, local copies, waits for them, and re-layouts, expert_slots(): jnp.zeros((capacity + 1,), jnp.int32).at[placed].set(index_row)[:capacity]  17.7 us
    gather x5, local copies, waits for them, and re-layouts, gate_table(): chosen = jnp.take_along_axis(logits, routes, axis=1)  13.7 us
    gather x4, local copies, waits for them, and re-layouts, local(): segment_ids[slot_tok][:, None] == segment_ids[None, :]  12.1 us
    gather x4, local copies, waits for them, and re-layouts, local(): gate_here = gates[slot_tok, expert] * is_valid.astype(jnp.float32)  10.7 us
  transfers between devices with their start and end apart: 3, of which 2 were waited for; matrix products, arithmetic and copies ran while one was open for 22% of the time, Pallas kernels for 0%

commit v1 on v0

--- a/solution.py
+++ b/solution.py
@@ -7,6 +7,12 @@
 HD = 128
 EA = 8
 PAGE = 128
+
+
+def gather_from_all(x, axis, dim):
+    length = lax.axis_size(axis)
+    repeats = [length if d == dim else 1 for d in range(x.ndim)]
+    return lax.all_to_all(jnp.tile(x, repeats), axis, split_axis=dim, concat_axis=dim, tiled=True)
 
 
 def swapped(array, axis, bit):
@@ -91,7 +97,7 @@
     device_index = lax.axis_index("tensor")
     token_count = routes.shape[0]
     capacity = 3 * token_count // 8
-    normed = lax.all_gather(normalize(hidden, norm_gain), "tensor", axis=0, tiled=True)
+    normed = gather_from_all(normalize(hidden, norm_gain), "tensor", 0)
     gates = gate_table(normed, router_weight, routes)
     positions = positions_of(segment_ids)
     kv_width = kv_weight.shape[1]

time: 498 us -> 535 us (1.074)
  local copies, waits for them, and re-layouts: 182 us -> 195 us
  waiting for transfers between devices: 243 us -> 256 us
  starting transfers between devices: 1.99 us -> 11.7 us
    all_to_all x0 -> x1, waiting for transfers between devices: none -> 40.2 us  [gather_from_all(): lax.all_to_all(jnp.tile(x, repeats), axis, split_axis=dim, concat_axis=di...]
    all_gather x1 -> x0, waiting for transfers between devices: 27.8 us -> none  [local(): lax.all_gather(normalize(hidden, norm_gain), 'tensor', axis=0, tiled=True)]
    all_to_all x0 -> x1, starting transfers between devices: none -> 11.6 us  [gather_from_all(): lax.all_to_all(jnp.tile(x, repeats), axis, split_axis=dim, concat_axis=di...]
    gather x4, local copies, waits for them, and re-layouts: 31.1 us -> 41.8 us  [local(): normed[slot_tok]]
  transfers between devices with their start and end apart: 3 -> 3, of which waited for: 2 -> 2; matrix products, arithmetic and copies ran while one was open for 22% -> 18% of each run, Pallas kernels for 0% -> 0%
where the time goes in v1:
time: 535 us; the launch traced here: 528 us
  waiting for transfers between devices  256 us (48%)
  local copies, waits for them, and re-layouts  195 us (36%)
  other arithmetic  25.7 us (5%)
  matrix products  24.5 us (5%)
  between operations  15.1 us (3%)
  starting transfers between devices  11.7 us (2%)
    reduce_scatter x1, waiting for transfers between devices, local(): lax.psum_scatter(jnp.dot(flat_spread, out_weight, preferred_element_type=...  216 us
    scatter x4, local copies, waits for them, and re-layouts, local(): spread = spread.at[target, :, expert_slot].set(gated, mode='drop')  78.1 us
    gather x4, local copies, waits for them, and re-layouts, local(): normed[slot_tok]  41.8 us
    all_to_all x1, waiting for transfers between devices, gather_from_all(): lax.all_to_all(jnp.tile(x, repeats), axis, split_axis=dim, concat_axis=di...  40.2 us
    scatter x4, local copies, waits for them, and re-layouts, expert_slots(): jnp.zeros((capacity + 1,), jnp.int32).at[placed].set(index_row)[:capacity]  17.6 us
    gather x5, local copies, waits for them, and re-layouts, gate_table(): chosen = jnp.take_along_axis(logits, routes, axis=1)  13.7 us
    gather x4, local copies, waits for them, and re-layouts, local(): segment_ids[slot_tok][:, None] == segment_ids[None, :]  11.9 us
    all_to_all x1, starting transfers between devices, gather_from_all(): lax.all_to_all(jnp.tile(x, repeats), axis, split_axis=dim, concat_axis=di...  11.6 us
  transfers between devices with their start and end apart: 3, of which 2 were waited for; matrix products, arithmetic and copies ran while one was open for 18% of the time, Pallas kernels for 0%

profile of v1, /device:TPU:8, one launch (start us, length us, event | category | flops | bytes accessed | tf_op | source)
XLA Modules:
  0.0 528.0 jit_solution(5204524239605948430)
XLA Ops:
  10.1 2.5 tile.2
  12.6 11.6 %all-to-all-start = ((bf16[32,32,2048]{2,1,0:T(8,128)(2,1)}), bf16[32,32,2048]{2,1,0:T(8,128)(2,1)}, u32[]{:S(2)}, u32[]{:S(2)}) async-start(bf16[32,32,2048]{2,1,0:T(8,128)(2,1)} %tile.2), calls=%async_computation | async-start | bytes 8388608 | tf_op jit(solution)/shard_map/all_to_all | solution.py:15
  27.3 4.3 scatter_custom_fusion.6
  32.9 3.0 gather_fusion.12
  38.0 4.3 scatter_custom_fusion.4
  45.5 2.9 gather_fusion.8
  50.2 4.3 scatter_custom_fusion.2
  57.6 3.0 gather_fusion.4
  61.2 4.7 scatter_custom_fusion
  68.9 3.0 gather_fusion
  71.9 4.0 copy.62
  81.1 40.2 %all-to-all-done = bf16[32,32,2048]{2,1,0:T(8,128)(2,1)} async-done(((bf16[32,32,2048]{2,1,0:T(8,128)(2,1)}), bf16[32,32,2048]{2,1,0:T(8,128)(2,1)}, u32[]{:S(2)}, u32[]{:S(2)}) %all-to-all-start) | async-done | bytes 4194336 | tf_op jit(solution)/shard_map/all_to_all | solution.py:15
  121.4 7.8 %gather_fusion.13 = bf16[384,2048]{1,0:T(8,128)(2,1)} fusion(bf16[1024,2048]{1,0:T(8,128)(2,1)} %bitcast.5, s32[1024]{0:T(1024)S(1)} %pad_clamp_fusion), kind=kCustom, calls=%fused_computation.13 | custom fusion | bytes 3147264 | tf_op jit(solution)/shard_map/gather | solution.py:127
  129.1 7.8 %gather_fusion.9 = bf16[384,2048]{1,0:T(8,128)(2,1)} fusion(bf16[1024,2048]{1,0:T(8,128)(2,1)} %bitcast.5, s32[1024]{0:T(1024)S(1)} %pad_clamp_fusion.1), kind=kCustom, calls=%fused_computation.9 | custom fusion | bytes 3147264 | tf_op jit(solution)/shard_map/gather | solution.py:127
  137.0 7.8 %gather_fusion.5 = bf16[384,2048]{1,0:T(8,128)(2,1)} fusion(bf16[1024,2048]{1,0:T(8,128)(2,1)} %bitcast.5, s32[1024]{0:T(1024)S(1)} %pad_clamp_fusion.2), kind=kCustom, calls=%fused_computation.5 | custom fusion | bytes 3147264 | tf_op jit(solution)/shard_map/gather | solution.py:127
  144.8 18.4 %gather_fusion.1 = bf16[384,2048]{1,0:T(8,128)(2,1)} fusion(bf16[1024,2048]{1,0:T(8,128)(2,1)} %bitcast.5, s32[1024]{0:T(1024)S(1)} %pad_clamp_fusion.3), kind=kCustom, calls=%fused_computation.1 | custom fusion | bytes 3147264 | tf_op jit(solution)/shard_map/gather | solution.py:127
  163.1 2.9 convolution_bitcast_fusion
  166.0 2.4 convolution_bitcast_fusion.1
  168.4 3.7 fusion.110
  174.1 3.4 fusion.111
  177.5 12.5 %gather_fusion.16 = f32[2048]{0:T(1024)S(1)} fusion(f32[1024,8]{0,1:T(8,128)S(1)} %fusion.111, s32[2048]{0:T(1024)S(1)} %reshape.1040), kind=kCustom, calls=%fused_computation.16 | custom fusion | bytes 32768 | tf_op jit(solution)/shard_map/jit(take_along_axis)/gather | solution.py:30
  190.8 2.7 gather_fusion.15
  194.2 2.7 gather_fusion.11
  197.6 2.7 gather_fusion.7
  200.9 2.7 gather_fusion.3
  204.3 2.1 convolution_bitcast_fusion.3
  218.2 19.2 %scatter_fusion = bf16[1024,4,128]{2,1,0:T(4,128)(2,1)S(1)} fusion(bf16[1024,4,128]{2,1,0:T(4,128)(2,1)S(1)} %broadcast.769, s32[384]{0:T(512)S(1)} %copy-done.6, bf16[384,128]{1,0:T(8,128)(2,1)S(1)} %fusion.12), kind=kCustom, calls=%fused_computation.18 | custom fusion | bytes 297984 | tf_op jit(solution)/shard_map/scatter | solution.py:141
  237.4 19.7 %scatter_fusion.1 = bf16[1024,4,128]{2,1,0:T(4,128)(2,1)S(1)} fusion(bf16[1024,4,128]{2,1,0:T(4,128)(2,1)S(1)} %scatter_fusion, s32[384]{0:T(512)S(1)} %copy-done.5, bf16[384,128]{1,0:T(8,128)(2,1)S(1)} %fusion.13), kind=kCustom, calls=%fused_computation.20 | custom fusion | bytes 297984 | tf_op jit(solution)/shard_map/scatter | solution.py:141
  257.1 19.7 %scatter_fusion.2 = bf16[1024,4,128]{2,1,0:T(4,128)(2,1)S(1)} fusion(bf16[1024,4,128]{2,1,0:T(4,128)(2,1)S(1)} %scatter_fusion.1, s32[384]{0:T(512)S(1)} %copy-done.4, bf16[384,128]{1,0:T(8,128)(2,1)S(1)} %fusion.14), kind=kCustom, calls=%fused_computation.22 | custom fusion | bytes 297984 | tf_op jit(solution)/shard_map/scatter | solution.py:141
  276.8 19.6 %scatter_fusion.3 = bf16[1024,4,128]{2,1,0:T(4,128)(2,1)S(1)} fusion(bf16[1024,4,128]{2,1,0:T(4,128)(2,1)S(1)} %scatter_fusion.2, s32[384]{0:T(512)S(1)} %copy-done.3, bf16[384,128]{1,0:T(8,128)(2,1)S(1)} %fusion.15), kind=kCustom, calls=%fused_computation.24 | custom fusion | bytes 297984 | tf_op jit(solution)/shard_map/scatter | solution.py:141
  296.4 4.3 convolution_convert_fusion
  303.3 216.1 %reduce-scatter.2.cloned.1.call-done = bf16[32,2048]{1,0:T(8,128)(2,1)} async-done(((bf16[1024,2048]{1,0:T(8,128)(2,1)}), bf16[32,2048]{1,0:T(8,128)(2,1)}) %reduce-scatter.2.cloned.1.call-update) | async-done | bytes 131088 | tf_op jit(solution)/shard_map/reduce_scatter | solution.py:143
  (181 shorter events, 47.2 us)
Async XLA Ops:
  7.2 289.2 %copy-start = (bf16[512,2048]{1,0:T(8,128)(2,1)S(1)}, bf16[512,2048]{1,0:T(8,128)(2,1)}, u32[]{:S(2)}) copy-start(bf16[512,2048]{1,0:T(8,128)(2,1)} %param.15) | copy-start | bytes 6291460
  12.6 11.7 %copy-start.19 = (s32[1024,2]{0,1:T(2,128)S(1)}, s32[1024,2]{0,1:T(2,128)}, u32[]{:S(2)}) copy-start(s32[1024,2]{0,1:T(2,128)} %param.16) | copy-start | bytes 24580
  12.6 14.2 %copy-start.1 = (s32[1024]{0:T(1024)S(1)}, s32[1024]{0:T(1024)}, u32[]{:S(2)}) copy-start(s32[1024]{0:T(1024)} %param.17) | copy-start | bytes 12292
  12.6 108.8 %all-to-all-start = ((bf16[32,32,2048]{2,1,0:T(8,128)(2,1)}), bf16[32,32,2048]{2,1,0:T(8,128)(2,1)}, u32[]{:S(2)}, u32[]{:S(2)}) async-start(bf16[32,32,2048]{2,1,0:T(8,128)(2,1)} %tile.2), calls=%async_computation | async-start | bytes 8388608 | tf_op jit(solution)/shard_map/all_to_all | solution.py:15
  24.2 495.2 %reduce-scatter.2.cloned.1.call-start = ((), (), s32[]{:S(2)}) async-start(), calls=%async_computation.2 | async-start | bytes 4325376 | tf_op jit(solution)/shard_map/reduce_scatter | solution.py:143
  81.1 91.0 %copy-start.26 = (f32[64]{0:T(128)}, f32[64]{0:T(128)S(1)}, u32[]{:S(2)}) copy-start(f32[64]{0:T(128)S(1)} %multiply_power_fusion) | copy-start | bytes 772
  163.1 2.9 copy-start.12
  166.0 2.4 copy-start.16
  172.1 2.0 copy-start.21
  174.1 35.9 %collective-permute-start = (bf16[1024,128]{0,1:T(8,128)(2,1)}, bf16[1024,128]{0,1:T(8,128)(2,1)}, u32[]{:S(2)}, u32[]{:S(2)}) collective-permute-start(bf16[1024,128]{0,1:T(8,128)(2,1)} %fusion.18), channel_id=1, source_target_pairs={{0,1},{1,0},{2,3},{3,2},{4,5},{5,4},{6,7},{7,6},{8,9},{9,8},{10,11... | collective-permute-start | bytes 786440 | tf_op jit(solution)/shard_map/ppermute | solution.py:19
  177.5 13.2 %copy-start.20 = (s32[1024,2]{0,1:T(2,128)S(1)}, s32[1024,2]{0,1:T(2,128)}, u32[]{:S(2)}) copy-start(s32[1024,2]{0,1:T(2,128)} %param.16) | copy-start | bytes 24580
  177.5 13.3 %copy-start.7 = (s32[384]{0:T(512)S(1)}, s32[384]{0:T(512)}, u32[]{:S(2)}) copy-start(s32[384]{0:T(512)} %get-tuple-element.28) | copy-start | bytes 4612
  190.5 3.7 copy-start.8
  193.5 4.1 copy-start.9
  196.9 4.0 copy-start.10
  203.6 2.8 copy-start.25
  203.6 2.8 copy-start.27
  203.6 3.3 copy-start.11
  206.5 2.2 copy-start.17
  206.5 2.2 copy-start.18
  206.5 2.2 copy-start.22
  206.5 2.2 copy-start.23
  206.5 2.2 copy-start.24
  208.7 2.7 copy-start.2
  208.7 2.7 copy-start.28
  208.7 2.7 copy-start.32
  217.9 19.5 %copy-start.5 = (s32[384]{0:T(512)S(1)}, s32[384]{0:T(512)}, u32[]{:S(2)}) copy-start(s32[384]{0:T(512)} %fusion.83) | copy-start | bytes 4612
  218.2 38.9 %copy-start.4 = (s32[384]{0:T(512)S(1)}, s32[384]{0:T(512)}, u32[]{:S(2)}) copy-start(s32[384]{0:T(512)} %fusion.85) | copy-start | bytes 4612
  237.4 39.4 %copy-start.3 = (s32[384]{0:T(512)S(1)}, s32[384]{0:T(512)}, u32[]{:S(2)}) copy-start(s32[384]{0:T(512)} %fusion.87) | copy-start | bytes 4612
  300.7 1.8 copy-start.15
  300.7 218.6 %copy-start.13 = (bf16[32,2048]{1,0:T(8,128)(2,1)S(1)}, bf16[32,2048]{1,0:T(8,128)(2,1)}, u32[]{:S(2)}) copy-start(bf16[32,2048]{1,0:T(8,128)(2,1)} %param.10) | copy-start | bytes 393220
  303.3 217.7 %copy-start.14 = (bf16[16,128,128]{2,1,0:T(8,128)(2,1)}, bf16[16,128,128]{2,1,0:T(8,128)(2,1)S(1)}, u32[]{:S(2)}) copy-start(bf16[16,128,128]{2,1,0:T(8,128)(2,1)S(1)} %scatter_fusion.4) | copy-start | bytes 1572868
  (8 other events, 5.4 us)
Sparse Core Ops, SparseCore 0:
  300.8 218.4 reduce-scatter.1
